TPU v7x, 1024 devices: a whole 4x4x32 slice. The times are simulated.
1024 devices in a mesh: wide: 64 (over z, core), rep: 16 (over x, y).
Axes of the slice: x: 4, y: 4, z: 32, core: 2. Of those that a mesh axis runs over, the one named last changes fastest.
Arguments:
- amplitudes: bfloat16 [64, 80, 128, 128], P(None, 'rep', 'wide'), may hold values from -6 to 6
- integrals: bfloat16 [80, 128, 80, 128], P('rep'), may hold values from -0.109375 to 0.109375
- occ_irrep: int32 [80], replicated, may hold values from 0 to 7
- vir_count: int32 [8], replicated, may hold values from 1 to 128, 600 in all
Outputs:
- cycle_block: bfloat16 [64, 128, 80, 128], P('wide', None, 'rep')
Inputs may be any that keep to these rules, and one draw needn't show every extreme that they name: `vir_count`: the 8 counts sum to 600; the largest is exactly 128.
All inputs are finite; a program needn't handle non-finite values.
Results may differ from a plain program's by a relative error of at most 0.017.
Values may be sent and summed in bfloat16 or wider, within the bound.
A program may use at most 64 MiB of HBM per device.

v0:
```python
import jax
import jax.numpy as jnp
from jax import lax
from jax.sharding import PartitionSpec as P

SYM = 3


def irrep_counts(occ_irrep, vir_count, first_row, row_count):
    labels = lax.dynamic_slice_in_dim(occ_irrep, first_row, row_count, 0)
    target = jnp.bitwise_xor(labels, SYM)
    irreps = jnp.arange(vir_count.shape[0], dtype=jnp.int32)
    picked = jnp.where(target[:, None] == irreps[None, :], vir_count[None, :], 0)
    return jnp.sum(picked, axis=1)


def replica_sum(partial_value, col_share):
    summed = lax.psum(partial_value.astype(jnp.bfloat16), "rep").astype(jnp.float32)
    return lax.dynamic_slice_in_dim(summed, lax.axis_index("rep") * col_share, col_share, 2)


def body(amplitudes, integrals, occ_irrep, vir_count):
    wide_index = lax.axis_index("wide")
    rep_index = lax.axis_index("rep")
    occ_block = amplitudes.shape[1]
    slot_count = amplitudes.shape[3]
    vir_slots = jnp.arange(slot_count, dtype=jnp.int32)
    col_share = integrals.shape[2] // lax.axis_size("rep")
    k_counts = irrep_counts(occ_irrep, vir_count, rep_index * occ_block, occ_block)
    c_valid = k_counts[:, None] > vir_slots[None, :]
    j_counts = irrep_counts(occ_irrep, vir_count, rep_index * col_share, col_share)
    b_valid = (j_counts[:, None] > vir_slots[None, :]).astype(jnp.float32)
    zero_value = jnp.zeros((), amplitudes.dtype)
    pair_amps = lax.all_to_all(amplitudes, "wide", split_axis=0, concat_axis=2, tiled=True)
    masked = jnp.where(c_valid[None, :, None, :], pair_amps, zero_value)
    partial_value = jnp.einsum(
        "ikac,kcjb->iajb", masked, integrals, preferred_element_type=jnp.float32
    )
    reduced = replica_sum(partial_value, col_share)
    row_total = pair_amps.shape[0]
    i_counts = irrep_counts(occ_irrep, vir_count, wide_index * row_total, row_total)
    a_valid = (i_counts[:, None] > vir_slots[None, :]).astype(jnp.float32)
    result = reduced * a_valid[:, :, None, None] * b_valid[None, None, :, :]
    return result.astype(jnp.bfloat16)


def solution(mesh):
    in_specs = (P(None, "rep", "wide", None), P("rep", None, None, None), P(), P())
    out_specs = P("wide", None, "rep", None)
    return jax.shard_map(body, mesh=mesh, in_specs=in_specs, out_specs=out_specs, check_vma=False)
```

profile of v0, /device:TPU:1, one launch (start us, length us, event | category | flops | bytes accessed | tf_op | source)
XLA Modules:
  0.0 234.5 jit_solution(2785868177294237508)
XLA Ops:
  6.5 30.4 %all-to-all-start = ((bf16[64,5,2,128]{3,2,1,0:T(2,128)(2,1)}), bf16[64,5,2,128]{3,2,1,0:T(2,128)(2,1)S(1)}, u32[]{:S(2)}, u32[]{:S(2)}) async-start(bf16[64,5,2,128]{3,2,1,0:T(2,128)(2,1)} %param.4), calls=%async_computation | async-start | bytes 327680 | tf_op jit(solution)/shard_map/all_to_all | solution.py:34
  36.9 0.0 all-reduce.2.cloned.1.call-start
  37.0 0.7 dynamic-slice_xor_fusion
  37.7 0.8 select_reduce_fusion
  38.6 0.1 fusion.11
  38.6 31.9 %all-to-all-done = bf16[64,5,2,128]{3,2,1,0:T(2,128)(2,1)S(1)} async-done(((bf16[64,5,2,128]{3,2,1,0:T(2,128)(2,1)}), bf16[64,5,2,128]{3,2,1,0:T(2,128)(2,1)S(1)}, u32[]{:S(2)}, u32[]{:S(2)}) %all-to-all-start) | async-done | bytes 163872 | tf_op jit(solution)/shard_map/all_to_all | solution.py:34
  70.6 0.1 copy.8
  70.7 0.0 copy-start
  70.7 0.0 copy-start.1
  70.7 8.6 %fusion.2 = bf16[1,128,80,128]{3,1,2,0:T(8,128)(2,1)} fusion(bf16[5,128,80,128]{3,2,1,0:T(8,128)(2,1)} %param.5, bf16[5,128,128]{2,1,0:T(8,128)(2,1)S(1)} %bitcast.16, pred[5,128]{1,0:T(8,128)(4,1)S(1)} %get-tuple-element.6), kind=kOutput, calls=%fused_computation.3 | convolution fusion | flops 1679114240 | bytes 15893120 | tf_op jit(solution)/shard_map/ikac,kcjb->iajb/dot_general | solution.py:36
  79.4 0.0 all-reduce.2.cloned.1.call-update
  79.4 0.0 copy-done
  79.4 0.6 dynamic_slice.12
  80.6 0.0 copy-done.1
  80.6 0.7 fusion.9
  81.3 0.6 compare_convert_fusion
  81.9 144.1 %all-reduce.2.cloned.1.call-done = bf16[1,128,80,128]{3,1,2,0:T(8,128)(2,1)} async-done(((bf16[1,128,80,128]{3,1,2,0:T(8,128)(2,1)}), bf16[1,128,80,128]{3,1,2,0:T(8,128)(2,1)}) %all-reduce.2.cloned.1.call-update) | async-done | bytes 2621456 | tf_op jit(solution)/shard_map/psum | solution.py:18
  226.0 1.7 multiply_convert_fusion
Async XLA Ops:
  6.5 64.0 %all-to-all-start = ((bf16[64,5,2,128]{3,2,1,0:T(2,128)(2,1)}), bf16[64,5,2,128]{3,2,1,0:T(2,128)(2,1)S(1)}, u32[]{:S(2)}, u32[]{:S(2)}) async-start(bf16[64,5,2,128]{3,2,1,0:T(2,128)(2,1)} %param.4), calls=%async_computation | async-start | bytes 327680 | tf_op jit(solution)/shard_map/all_to_all | solution.py:34
  36.9 189.1 %all-reduce.2.cloned.1.call-start = ((), (), s32[]{:S(2)}) async-start(), calls=%async_computation.1 | async-start | bytes 5242880 | tf_op jit(solution)/shard_map/psum | solution.py:18
  70.7 8.7 %copy-start = (s32[80]{0:T(128)S(1)}, s32[80]{0:T(128)}, u32[]{:S(2)}) copy-start(s32[80]{0:T(128)} %param.6) | copy-start | bytes 964
  70.7 9.9 %copy-start.1 = (s32[8]{0:T(128)S(1)}, s32[8]{0:T(128)}, u32[]{:S(2)}) copy-start(s32[8]{0:T(128)} %param.7) | copy-start | bytes 100
Sparse Core Ops, SparseCore 0:
  79.5 146.4 all-reduce.1
where the time goes:
time: 235 us
  waiting for transfers between devices  176 us (75%)
  starting transfers between devices  30.4 us (13%)
  between operations  14.1 us (6%)
  matrix products  8.64 us (4%)
  other arithmetic  4.63 us (2%)
    psum x1, waiting for transfers between devices, replica_sum(): lax.psum(partial_value.astype(jnp.bfloat16), 'rep').astype(jnp.float32)  144 us
    all_to_all x1, waiting for transfers between devices, body(): lax.all_to_all(amplitudes, 'wide', split_axis=0, concat_axis=2, tiled=True)  31.9 us
    all_to_all x1, starting transfers between devices, body(): lax.all_to_all(amplitudes, 'wide', split_axis=0, concat_axis=2, tiled=True)  30.4 us
    dot_general x1, matrix products, body(): jnp.einsum('ikac,kcjb->iajb', masked, integrals, preferred_element_type=j...  8.64 us
  transfers between devices with their start and end apart: 2, of which 2 were waited for; matrix products, arithmetic and copies ran while one was open for 2% of the time, Pallas kernels for 0%

commit v1 on v0

v1 whole, which is shorter than its diff:
```python
import jax
import jax.numpy as jnp
from jax import lax
from jax.experimental import pallas as pl
from jax.experimental.pallas import tpu as pltpu
from jax.sharding import PartitionSpec as P

SYM = 3
MESH = pl.DeviceIdType.MESH
F32 = jnp.float32
BF16 = jnp.bfloat16

WIDE = 64
GROUP = 8
SLOTS = 128
SIDE = 4
K_LOCAL = 5
J_LOCAL = 5
CHUNKS = ((-1, 0, 1, 2), (3, 4, 5, 6))


def to_f32(value):
    return value.astype(F32)


def kernel(
    amps_hbm, ints_hbm, occ_ref, vir_ref, out_ref,
    amps, slots_in, raw, weights, rows, part, first_in, second_in, mid, third_in, fourth_in,
    load_sems, own_sem, spread_send, spread_recv, main_send, first_recv, second_recv,
    side_send, third_recv, fourth_recv,
):
    wide = lax.axis_index("wide")
    rep = lax.axis_index("rep")
    x, y = rep // SIDE, rep % SIDE
    group = wide // GROUP

    amps_load = pltpu.make_async_copy(amps_hbm, amps, load_sems.at[K_LOCAL])
    amps_load.start()
    int_loads = [
        pltpu.make_async_copy(ints_hbm.at[k], raw.at[k], load_sems.at[k])
        for k in range(K_LOCAL)
    ]
    for load in int_loads:
        load.start()

    def along(axis, step):
        if axis == 0:
            other = lax.rem(x + step + SIDE, SIDE) * SIDE + y
        else:
            other = x * SIDE + lax.rem(y + step + SIDE, SIDE)
        return {"wide": wide, "rep": other}

    barrier = pltpu.get_barrier_semaphore()

    def greet(step, carry):
        peer = lax.rem(wide + step, WIDE)
        pl.semaphore_signal(
            barrier, inc=1, device_id={"wide": peer, "rep": rep}, device_id_type=MESH
        )
        return carry

    for axis in range(2):
        for step in (1, -1):
            pl.semaphore_signal(
                barrier, inc=1, device_id=along(axis, step), device_id_type=MESH
            )
    lax.fori_loop(1, WIDE, greet, 0)
    amps_load.wait()
    own = pltpu.make_async_copy(amps.at[wide], slots_in.at[wide], own_sem)
    own.start()
    pl.semaphore_wait(barrier, WIDE - 1 + 4)

    def spread(chunk, first, last, peer_of):
        def send(step, carry):
            peer = peer_of(step)
            pltpu.make_async_remote_copy(
                src_ref=amps.at[peer],
                dst_ref=slots_in.at[wide],
                send_sem=spread_send,
                recv_sem=spread_recv.at[chunk],
                device_id={"wide": peer, "rep": rep},
                device_id_type=MESH,
            ).start()
            return carry

        lax.fori_loop(first, last, send, 0)

    for chunk, sources in enumerate(CHUNKS):
        for source in sorted(sources, key=lambda s: min(s % 8, -s % 8)):
            base = lax.rem(group + (GROUP - source) + GROUP, GROUP) * GROUP
            if source == 0:
                inside = wide - group * GROUP
                spread(chunk, 1, GROUP, lambda s: base + lax.rem(inside + s, GROUP))
            else:
                spread(chunk, 0, GROUP, lambda s, base=base: base + s)

    for k in range(K_LOCAL):
        int_loads[k].wait()

        def turn(step, carry, k=k):
            c = pl.multiple_of(step * 16, 16)
            to = pl.multiple_of(k * SLOTS + step * 16, 16)
            for q in range(5):
                block = raw[k, pl.ds(c, 16), 16 * q : 16 * q + 16, :]
                weights[16 * q : 16 * q + 16, pl.ds(to, 16), :] = jnp.swapaxes(block, 0, 1)
            return carry

        lax.fori_loop(0, SLOTS // 16, turn, 0)

    lane = lax.broadcasted_iota(jnp.int32, (16, SLOTS), 1)
    row = lax.broadcasted_iota(jnp.int32, (16, SLOTS), 0)

    def count_of(orbital):
        return vir_ref[jnp.bitwise_xor(occ_ref[orbital], SYM)]

    def absolute(chunk, place):
        return lax.rem(group + CHUNKS[chunk][place] + GROUP, GROUP)

    def wait_slots(chunk):
        many = 31 if chunk == 0 else 32
        pltpu.make_async_remote_copy(
            src_ref=amps.at[pl.ds(0, many)],
            dst_ref=slots_in.at[pl.ds(0, many)],
            send_sem=spread_send,
            recv_sem=spread_recv.at[chunk],
            device_id=along(0, 1),
            device_id_type=MESH,
        ).wait_recv()
        if chunk == 0:
            own.wait()

    def gather_rows(chunk):
        for k in range(K_LOCAL):
            valid = lane < count_of(rep * K_LOCAL + k)
            for place in range(4):
                at = pl.multiple_of(absolute(chunk, place) * GROUP, GROUP)
                block = slots_in[pl.ds(at, GROUP), k, :, :].reshape(16, SLOTS)
                rows[chunk, 16 * place : 16 * place + 16, SLOTS * k : SLOTS * k + SLOTS] = (
                    jnp.where(valid, to_f32(block), 0.0).astype(BF16)
                )

    sent = []

    def send(src, dst, sems, index, recv, device):
        copy = pltpu.make_async_remote_copy(
            src_ref=src,
            dst_ref=dst,
            send_sem=sems.at[index],
            recv_sem=recv,
            device_id=device,
            device_id_type=MESH,
        )
        copy.start()
        sent.append(copy)
        return copy

    def multiply(chunk):
        for dx in (2, 1, 3, 0):

            def pair(t, carry, dx=dx):
                pieces = []
                ways = (2 + t, 1 - t)
                for dy in ways:
                    target = lax.rem(x + dx, SIDE) * SIDE + lax.rem(y + dy, SIDE)
                    pieces += [weights[target * J_LOCAL + j] for j in range(J_LOCAL)]
                product = jnp.dot(
                    rows[chunk], jnp.concatenate(pieces, axis=1), preferred_element_type=F32
                ).astype(BF16)
                for n, dy in enumerate(ways):
                    for j in range(J_LOCAL):
                        at = (n * J_LOCAL + j) * SLOTS
                        part[chunk, 0, dx, dy, j] = product[:32, at : at + SLOTS]
                        part[chunk, 1, dy, dx, j] = product[32:, at : at + SLOTS]
                return carry

            lax.fori_loop(0, 2, pair, 0)
            base = chunk * 16
            if dx == 2:
                for d, half in ((0, 0), (1, 2)):
                    send(
                        part.at[chunk, 0, 2, pl.ds(half, 2)], first_in.at[chunk, 0, d],
                        main_send, base + d, first_recv.at[chunk, 0, d], along(0, 1 - 2 * d),
                    )
            if dx in (1, 3):
                d, half = (0, 2) if dx == 1 else (1, 0)
                send(
                    part.at[chunk, 0, dx, pl.ds(half, 2)],
                    second_in.at[chunk, 0, d, pl.ds(half, 2)],
                    main_send, base + 2 + d, second_recv.at[chunk, 0, d, 0], along(0, 1 - 2 * d),
                )
            d = 0 if dx < 2 else 1
            send(
                part.at[chunk, 1, 2, dx], first_in.at[chunk, 1, d, dx % 2],
                main_send, base + 4 + dx, first_recv.at[chunk, 1, d], along(1, 1 - 2 * d),
            )
            send(
                part.at[chunk, 1, 1 if d else 3, dx], second_in.at[chunk, 1, 1 - d, dx],
                main_send, base + 8 + dx, second_recv.at[chunk, 1, 1 - d, 0], along(1, 2 * d - 1),
            )

    def wait_for(buffer, sem):
        pltpu.make_async_remote_copy(
            src_ref=buffer, dst_ref=buffer, send_sem=own_sem, recv_sem=sem,
            device_id=along(0, 1), device_id_type=MESH,
        ).wait_recv()

    def pass_on(chunk):
        for way in range(2):
            for d in range(2):
                dp, half = (1, 0) if d == 0 else (3, 2)
                wait_for(first_in.at[chunk, way, d], first_recv.at[chunk, way, d])
                part[chunk, way, dp, half : half + 2] = (
                    to_f32(part[chunk, way, dp, half : half + 2]) + to_f32(first_in[chunk, way, d])
                ).astype(BF16)
                send(
                    part.at[chunk, way, dp, pl.ds(half, 2)],
                    second_in.at[chunk, way, d, pl.ds(half, 2)],
                    main_send, chunk * 16 + 12 + 2 * way + d,
                    second_recv.at[chunk, way, d, 1], along(way, 1 - 2 * d),
                )

    def turn_corner(chunk):
        for way in range(2):
            for d in range(2):
                for late in range(2):
                    half = 2 * ((1 - late + d) % 2)
                    wait_for(
                        second_in.at[chunk, way, d, pl.ds(half, 2)],
                        second_recv.at[chunk, way, d, late],
                    )
            for ds in (2, 1, 3, 0):
                total = (
                    to_f32(part[chunk, way, 0, ds])
                    + to_f32(second_in[chunk, way, 0, ds])
                    + to_f32(second_in[chunk, way, 1, ds])
                ).astype(BF16)
                mid[chunk, way, ds, 0] = total[:, :16]
                mid[chunk, way, ds, 1] = total[:, 16:]
                base = chunk * 12 + way * 6
                axis = 1 - way
                if ds == 2:
                    for d in range(2):
                        send(
                            mid.at[chunk, way, 2, d], third_in.at[chunk, way, d],
                            side_send, base + d, third_recv.at[chunk, way, d],
                            along(axis, 1 - 2 * d),
                        )
                if ds in (1, 3):
                    d, h = (0, 1) if ds == 1 else (1, 0)
                    send(
                        mid.at[chunk, way, ds, h], fourth_in.at[chunk, way, d, h],
                        side_send, base + 2 + d, fourth_recv.at[chunk, way, d, h],
                        along(axis, 1 - 2 * d),
                    )

    def pass_on_side(chunk):
        for way in range(2):
            for d in range(2):
                ds = 1 if d == 0 else 3
                wait_for(third_in.at[chunk, way, d], third_recv.at[chunk, way, d])
                mid[chunk, way, ds, d] = (
                    to_f32(mid[chunk, way, ds, d]) + to_f32(third_in[chunk, way, d])
                ).astype(BF16)
                send(
                    mid.at[chunk, way, ds, d], fourth_in.at[chunk, way, d, d],
                    side_send, chunk * 12 + way * 6 + 4 + d, fourth_recv.at[chunk, way, d, d],
                    along(1 - way, 1 - 2 * d),
                )

    def finish(chunk):
        row_count = count_of(wide)
        for way in range(2):
            for d in range(2):
                for h in range(2):
                    wait_for(fourth_in.at[chunk, way, d, h], fourth_recv.at[chunk, way, d, h])
            for h in range(2):
                at = pl.multiple_of(absolute(chunk, 2 * way + h) * 16, 16)
                for j in range(J_LOCAL):
                    total = (
                        to_f32(mid[chunk, way, 0, h, j])
                        + to_f32(fourth_in[chunk, way, 0, h, j])
                        + to_f32(fourth_in[chunk, way, 1, h, j])
                    )
                    valid = (row + at < row_count) & (lane < count_of(rep * J_LOCAL + j))
                    out_ref[j, pl.ds(at, 16), :] = jnp.where(valid, total, 0.0).astype(BF16)

    wait_slots(0)
    gather_rows(0)
    multiply(0)
    pass_on(0)
    turn_corner(0)
    wait_slots(1)
    gather_rows(1)
    multiply(1)
    pass_on_side(0)
    pass_on(1)
    finish(0)
    turn_corner(1)
    pass_on_side(1)
    finish(1)

    pltpu.make_async_remote_copy(
        src_ref=amps.at[pl.ds(0, WIDE - 1)],
        dst_ref=slots_in.at[pl.ds(0, WIDE - 1)],
        send_sem=spread_send,
        recv_sem=spread_recv.at[0],
        device_id=along(0, 1),
        device_id_type=MESH,
    ).wait_send()
    for copy in sent:
        copy.wait_send()


def body(amplitudes, integrals, occ_irrep, vir_count):
    dma = pltpu.SemaphoreType.DMA
    out = pl.pallas_call(
        kernel,
        out_shape=jax.ShapeDtypeStruct((J_LOCAL, SLOTS, SLOTS), BF16),
        in_specs=[
            pl.BlockSpec(memory_space=pl.ANY),
            pl.BlockSpec(memory_space=pl.ANY),
            pl.BlockSpec(memory_space=pltpu.SMEM),
            pl.BlockSpec(memory_space=pltpu.SMEM),
        ],
        out_specs=pl.BlockSpec(memory_space=pltpu.VMEM),
        scratch_shapes=[
            pltpu.VMEM((WIDE, K_LOCAL, 2, SLOTS), BF16),
            pltpu.VMEM((WIDE, K_LOCAL, 2, SLOTS), BF16),
            pltpu.VMEM((K_LOCAL, SLOTS, 80, SLOTS), BF16),
            pltpu.VMEM((80, K_LOCAL * SLOTS, SLOTS), BF16),
            pltpu.VMEM((2, 64, K_LOCAL * SLOTS), BF16),
            pltpu.VMEM((2, 2, 4, 4, J_LOCAL, 32, SLOTS), BF16),
            pltpu.VMEM((2, 2, 2, 2, J_LOCAL, 32, SLOTS), BF16),
            pltpu.VMEM((2, 2, 2, 4, J_LOCAL, 32, SLOTS), BF16),
            pltpu.VMEM((2, 2, 4, 2, J_LOCAL, 16, SLOTS), BF16),
            pltpu.VMEM((2, 2, 2, J_LOCAL, 16, SLOTS), BF16),
            pltpu.VMEM((2, 2, 2, 2, J_LOCAL, 16, SLOTS), BF16),
            dma((K_LOCAL + 1,)),
            dma,
            dma,
            dma((2,)),
            dma((32,)),
            dma((2, 2, 2)),
            dma((2, 2, 2, 2)),
            dma((24,)),
            dma((2, 2, 2)),
            dma((2, 2, 2, 2)),
        ],
        compiler_params=pltpu.CompilerParams(
            collective_id=0, has_side_effects=True, vmem_limit_bytes=52 * 2**20
        ),
        cost_estimate=pl.CostEstimate(
            flops=2 * 128 * 640 * 10240, bytes_accessed=14 * 2**20, transcendentals=0
        ),
    )(amplitudes, integrals, occ_irrep, vir_count)
    return out.transpose(1, 0, 2)[None]


def solution(mesh):
    in_specs = (P(None, "rep", "wide", None), P("rep", None, None, None), P(), P())
    out_specs = P("wide", None, "rep", None)
    return jax.shard_map(body, mesh=mesh, in_specs=in_specs, out_specs=out_specs, check_vma=False)
```

time: 235 us -> 77.5 us (0.33)
  the two profiles are of different devices: /device:TPU:1 before, /device:TPU:8 now
where the time goes in v1:
time: 77.5 us; the launch traced here: 77.4 us
  Pallas kernels  74.5 us (96%)
  local copies, waits for them, and re-layouts  2.89 us (4%)
    pallas_call x1, Pallas kernels, body(): pl.pallas_call(kernel, out_shape=jax.ShapeDtypeStruct((J_LOCAL, SLOTS, SL...  74.5 us
    unnamed x7, local copies, waits for them, and re-layouts  2.89 us

profile of v1, /device:TPU:8, one launch (start us, length us, event | category | flops | bytes accessed | tf_op | source)
XLA Modules:
  0.0 77.4 jit_solution(130729772971086348)
XLA Ops:
  0.0 0.0 copy-start
  0.0 0.9 %copy-done = bf16[64,5,2,128]{3,2,1,0:T(2,128)(2,1)S(1)} copy-done((bf16[64,5,2,128]{3,2,1,0:T(2,128)(2,1)S(1)}, bf16[64,5,2,128]{3,2,1,0:T(2,128)(2,1)}, u32[]{:S(2)}) %copy-start) | copy-done | bytes 163864
  0.9 0.0 copy-start.1
  0.9 0.7 copy-done.1
  1.6 0.0 copy-start.2
  1.6 0.7 copy-done.2
  2.2 74.5 %shard_map.46 = bf16[5,128,128]{2,1,0:T(8,128)(2,1)S(1)} custom-call(bf16[64,5,2,128]{3,2,1,0:T(2,128)(2,1)S(1)} %copy-done, bf16[5,128,80,128]{3,2,1,0:T(8,128)(2,1)} %ints_hbm.1, s32[80]{0:T(128)S(1)} %copy-done.1, s32[8]{0:T(128)S(1)} %copy-done.2), custom_call_target="tpu_custom_call" | custom-call | flops 1677721600 | bytes 14680064 | tf_op jit(solution)/shard_map/pallas_call | solution.py:316
  76.7 0.7 copy.6
Async XLA Ops:
  0.0 0.9 %copy-start = (bf16[64,5,2,128]{3,2,1,0:T(2,128)(2,1)S(1)}, bf16[64,5,2,128]{3,2,1,0:T(2,128)(2,1)}, u32[]{:S(2)}) copy-start(bf16[64,5,2,128]{3,2,1,0:T(2,128)(2,1)} %amps_hbm.1) | copy-start | bytes 491524
  0.9 0.7 copy-start.1
  1.6 0.7 copy-start.2

commit v2 on v1

--- a/solution.py
+++ b/solution.py
@@ -16,7 +16,7 @@
 SIDE = 4
 K_LOCAL = 5
 J_LOCAL = 5
-CHUNKS = ((-1, 0, 1, 2), (3, 4, 5, 6))
+CHUNKS = ((4, 3, -3, -2), (2, 1, -1, 0))
 
 
 def to_f32(value):
@@ -24,8 +24,8 @@
 
 
 def kernel(
-    amps_hbm, ints_hbm, occ_ref, vir_ref, out_ref,
-    amps, slots_in, raw, weights, rows, part, first_in, second_in, mid, third_in, fourth_in,
+    amps_hbm, ints_hbm, occ_hbm, vir_hbm, out_ref,
+    occ_ref, vir_ref, amps, blocks, blocks_in, raw, weights, rows, part, first_in, second_in, mid, third_in, fourth_in,
     load_sems, own_sem, spread_send, spread_recv, main_send, first_recv, second_recv,
     side_send, third_recv, fourth_recv,
 ):
@@ -36,6 +36,12 @@
 
     amps_load = pltpu.make_async_copy(amps_hbm, amps, load_sems.at[K_LOCAL])
     amps_load.start()
+    label_loads = [
+        pltpu.make_async_copy(occ_hbm, occ_ref, load_sems.at[K_LOCAL + 1]),
+        pltpu.make_async_copy(vir_hbm, vir_ref, load_sems.at[K_LOCAL + 2]),
+    ]
+    for load in label_loads:
+        load.start()
     int_loads = [
         pltpu.make_async_copy(ints_hbm.at[k], raw.at[k], load_sems.at[k])
         for k in range(K_LOCAL)
@@ -53,7 +59,7 @@
     barrier = pltpu.get_barrier_semaphore()
 
     def greet(step, carry):
-        peer = lax.rem(wide + step, WIDE)
+        peer = lax.rem(wide + WIDE // 2 + (1 - 2 * (step % 2)) * (step // 2) + WIDE, WIDE)
         pl.semaphore_signal(
             barrier, inc=1, device_id={"wide": peer, "rep": rep}, device_id_type=MESH
         )
@@ -65,35 +71,6 @@
                 barrier, inc=1, device_id=along(axis, step), device_id_type=MESH
             )
     lax.fori_loop(1, WIDE, greet, 0)
-    amps_load.wait()
-    own = pltpu.make_async_copy(amps.at[wide], slots_in.at[wide], own_sem)
-    own.start()
-    pl.semaphore_wait(barrier, WIDE - 1 + 4)
-
-    def spread(chunk, first, last, peer_of):
-        def send(step, carry):
-            peer = peer_of(step)
-            pltpu.make_async_remote_copy(
-                src_ref=amps.at[peer],
-                dst_ref=slots_in.at[wide],
-                send_sem=spread_send,
-                recv_sem=spread_recv.at[chunk],
-                device_id={"wide": peer, "rep": rep},
-                device_id_type=MESH,
-            ).start()
-            return carry
-
-        lax.fori_loop(first, last, send, 0)
-
-    for chunk, sources in enumerate(CHUNKS):
-        for source in sorted(sources, key=lambda s: min(s % 8, -s % 8)):
-            base = lax.rem(group + (GROUP - source) + GROUP, GROUP) * GROUP
-            if source == 0:
-                inside = wide - group * GROUP
-                spread(chunk, 1, GROUP, lambda s: base + lax.rem(inside + s, GROUP))
-            else:
-                spread(chunk, 0, GROUP, lambda s, base=base: base + s)
-
     for k in range(K_LOCAL):
         int_loads[k].wait()
 
@@ -107,34 +84,23 @@
 
         lax.fori_loop(0, SLOTS // 16, turn, 0)
 
+    for load in label_loads:
+        load.wait()
     lane = lax.broadcasted_iota(jnp.int32, (16, SLOTS), 1)
     row = lax.broadcasted_iota(jnp.int32, (16, SLOTS), 0)
 
     def count_of(orbital):
         return vir_ref[jnp.bitwise_xor(occ_ref[orbital], SYM)]
 
-    def absolute(chunk, place):
+    def target_group(chunk, place):
         return lax.rem(group + CHUNKS[chunk][place] + GROUP, GROUP)
-
-    def wait_slots(chunk):
-        many = 31 if chunk == 0 else 32
-        pltpu.make_async_remote_copy(
-            src_ref=amps.at[pl.ds(0, many)],
-            dst_ref=slots_in.at[pl.ds(0, many)],
-            send_sem=spread_send,
-            recv_sem=spread_recv.at[chunk],
-            device_id=along(0, 1),
-            device_id_type=MESH,
-        ).wait_recv()
-        if chunk == 0:
-            own.wait()
 
     def gather_rows(chunk):
         for k in range(K_LOCAL):
             valid = lane < count_of(rep * K_LOCAL + k)
             for place in range(4):
-                at = pl.multiple_of(absolute(chunk, place) * GROUP, GROUP)
-                block = slots_in[pl.ds(at, GROUP), k, :, :].reshape(16, SLOTS)
+                at = pl.multiple_of(target_group(chunk, place) * GROUP, GROUP)
+                block = amps[pl.ds(at, GROUP), k, :, :].reshape(16, SLOTS)
                 rows[chunk, 16 * place : 16 * place + 16, SLOTS * k : SLOTS * k + SLOTS] = (
                     jnp.where(valid, to_f32(block), 0.0).astype(BF16)
                 )
@@ -267,46 +233,83 @@
                     along(1 - way, 1 - 2 * d),
                 )
 
-    def finish(chunk):
-        row_count = count_of(wide)
+    def spread(chunk):
         for way in range(2):
             for d in range(2):
                 for h in range(2):
                     wait_for(fourth_in.at[chunk, way, d, h], fourth_recv.at[chunk, way, d, h])
             for h in range(2):
-                at = pl.multiple_of(absolute(chunk, 2 * way + h) * 16, 16)
+                place = 2 * way + h
+                base = pl.multiple_of(target_group(chunk, place) * GROUP, GROUP)
                 for j in range(J_LOCAL):
                     total = (
                         to_f32(mid[chunk, way, 0, h, j])
                         + to_f32(fourth_in[chunk, way, 0, h, j])
                         + to_f32(fourth_in[chunk, way, 1, h, j])
                     )
-                    valid = (row + at < row_count) & (lane < count_of(rep * J_LOCAL + j))
-                    out_ref[j, pl.ds(at, 16), :] = jnp.where(valid, total, 0.0).astype(BF16)
-
-    wait_slots(0)
+                    total = jnp.where(lane < count_of(rep * J_LOCAL + j), total, 0.0)
+                    blocks[pl.ds(base, GROUP), j, :, :] = total.astype(BF16).reshape(GROUP, 2, SLOTS)
+                near = CHUNKS[chunk][place] == 0
+                inside = wide - group * GROUP
+
+                def push(step, carry, base=base, near=near):
+                    peer = base + (lax.rem(inside + step, GROUP) if near else step)
+                    pltpu.make_async_remote_copy(
+                        src_ref=blocks.at[peer],
+                        dst_ref=blocks_in.at[wide],
+                        send_sem=spread_send,
+                        recv_sem=spread_recv.at[chunk],
+                        device_id={"wide": peer, "rep": rep},
+                        device_id_type=MESH,
+                    ).start()
+                    return carry
+
+                lax.fori_loop(1 if near else 0, GROUP, push, 0)
+
+    def blocks_copy(many, sem):
+        return pltpu.make_async_remote_copy(
+            src_ref=blocks.at[pl.ds(0, many)],
+            dst_ref=blocks_in.at[pl.ds(0, many)],
+            send_sem=spread_send,
+            recv_sem=sem,
+            device_id=along(0, 1),
+            device_id_type=MESH,
+        )
+
+    def assemble(chunk):
+        blocks_copy(32 - chunk, spread_recv.at[chunk]).wait_recv()
+        row_count = count_of(wide)
+        for away in CHUNKS[chunk]:
+            source = lax.rem(group - away + GROUP, GROUP)
+            at = pl.multiple_of(source * GROUP, GROUP)
+            to = pl.multiple_of(source * 16, 16)
+            for j in range(J_LOCAL):
+                block = blocks_in[pl.ds(at, GROUP), j, :, :].reshape(16, SLOTS)
+                out_ref[j, pl.ds(to, 16), :] = jnp.where(
+                    row + to < row_count, to_f32(block), 0.0
+                ).astype(BF16)
+
+    amps_load.wait()
     gather_rows(0)
+    gather_rows(1)
+    pl.semaphore_wait(barrier, WIDE - 1 + 4)
     multiply(0)
     pass_on(0)
+    multiply(1)
     turn_corner(0)
-    wait_slots(1)
-    gather_rows(1)
-    multiply(1)
+    pass_on(1)
     pass_on_side(0)
-    pass_on(1)
-    finish(0)
+    spread(0)
     turn_corner(1)
     pass_on_side(1)
-    finish(1)
-
-    pltpu.make_async_remote_copy(
-        src_ref=amps.at[pl.ds(0, WIDE - 1)],
-        dst_ref=slots_in.at[pl.ds(0, WIDE - 1)],
-        send_sem=spread_send,
-        recv_sem=spread_recv.at[0],
-        device_id=along(0, 1),
-        device_id_type=MESH,
-    ).wait_send()
+    spread(1)
+    own = pltpu.make_async_copy(blocks.at[wide], blocks_in.at[wide], own_sem)
+    own.start()
+    assemble(0)
+    own.wait()
+    assemble(1)
+
+    blocks_copy(WIDE - 1, spread_recv.at[0]).wait_send()
     for copy in sent:
         copy.wait_send()
 
@@ -316,15 +319,13 @@
     out = pl.pallas_call(
         kernel,
         out_shape=jax.ShapeDtypeStruct((J_LOCAL, SLOTS, SLOTS), BF16),
-        in_specs=[
-            pl.BlockSpec(memory_space=pl.ANY),
-            pl.BlockSpec(memory_space=pl.ANY),
-            pl.BlockSpec(memory_space=pltpu.SMEM),
-            pl.BlockSpec(memory_space=pltpu.SMEM),
-        ],
+        in_specs=[pl.BlockSpec(memory_space=pltpu.HBM)] * 4,
         out_specs=pl.BlockSpec(memory_space=pltpu.VMEM),
         scratch_shapes=[
+            pltpu.SMEM((80,), jnp.int32),
+            pltpu.SMEM((8,), jnp.int32),
             pltpu.VMEM((WIDE, K_LOCAL, 2, SLOTS), BF16),
+            pltpu.VMEM((WIDE, J_LOCAL, 2, SLOTS), BF16),
             pltpu.VMEM((WIDE, K_LOCAL, 2, SLOTS), BF16),
             pltpu.VMEM((K_LOCAL, SLOTS, 80, SLOTS), BF16),
             pltpu.VMEM((80, K_LOCAL * SLOTS, SLOTS), BF16),
@@ -335,7 +336,7 @@
             pltpu.VMEM((2, 2, 4, 2, J_LOCAL, 16, SLOTS), BF16),
             pltpu.VMEM((2, 2, 2, J_LOCAL, 16, SLOTS), BF16),
             pltpu.VMEM((2, 2, 2, 2, J_LOCAL, 16, SLOTS), BF16),
-            dma((K_LOCAL + 1,)),
+            dma((K_LOCAL + 3,)),
             dma,
             dma,
             dma((2,)),
@@ -347,7 +348,7 @@
             dma((2, 2, 2, 2)),
         ],
         compiler_params=pltpu.CompilerParams(
-            collective_id=0, has_side_effects=True, vmem_limit_bytes=52 * 2**20
+            collective_id=0, has_side_effects=True, vmem_limit_bytes=63 * 2**20
         ),
         cost_estimate=pl.CostEstimate(
             flops=2 * 128 * 640 * 10240, bytes_accessed=14 * 2**20, transcendentals=0

time: 77.5 us -> 68.3 us (0.88)
  the two profiles are of different devices: /device:TPU:8 before, /device:TPU:1 now
where the time goes in v2:
time: 68.3 us; the launch traced here: 68.1 us
  Pallas kernels  66.5 us (97%)
  local copies, waits for them, and re-layouts  1.59 us (2%)
    pallas_call x1, Pallas kernels, body(): pl.pallas_call(kernel, out_shape=jax.ShapeDtypeStruct((J_LOCAL, SLOTS, SL...  66.5 us
    unnamed x1, local copies, waits for them, and re-layouts  1.59 us

profile of v2, /device:TPU:1, one launch (start us, length us, event | category | flops | bytes accessed | tf_op | source)
XLA Modules:
  0.0 68.1 jit_solution(10238307369724544868)
XLA Ops:
  0.0 66.5 %shard_map.46 = bf16[5,128,128]{2,1,0:T(8,128)(2,1)} custom-call(bf16[64,5,2,128]{3,2,1,0:T(2,128)(2,1)} %amps_hbm.1, bf16[5,128,80,128]{3,2,1,0:T(8,128)(2,1)} %ints_hbm.1, s32[80]{0:T(128)} %occ_hbm.1, s32[8]{0:T(128)} %vir_hbm.1), custom_call_target="tpu_custom_call" | custom-call | flops 1677721600 | bytes 14680064 | tf_op jit(solution)/shard_map/pallas_call | solution.py:319
  66.5 1.6 %copy.6 = bf16[1,128,5,128]{3,1,2,0:T(8,128)(2,1)} copy(bf16[1,128,5,128]{3,1,2,0:T(8,128)(2,1)} %bitcast.3) | data formatting | bytes 327680

commit v3 on v2

--- a/solution.py
+++ b/solution.py
@@ -16,7 +16,9 @@
 SIDE = 4
 K_LOCAL = 5
 J_LOCAL = 5
-CHUNKS = ((4, 3, -3, -2), (2, 1, -1, 0))
+SLABS = 5
+ORDER = (2, 3, 1, 0)
+CHUNKS = ((3, -3, 4, -2), (2, -1, 1, 0))
 
 
 def to_f32(value):
@@ -24,8 +26,8 @@
 
 
 def kernel(
-    amps_hbm, ints_hbm, occ_hbm, vir_hbm, out_ref,
-    occ_ref, vir_ref, amps, blocks, blocks_in, raw, weights, rows, part, first_in, second_in, mid, third_in, fourth_in,
+    amps_hbm, ints_hbm, occ_hbm, vir_hbm, blocks_in,
+    occ_ref, vir_ref, amps, blocks, raw, weights, rows, part, first_in, second_in, mid, third_in, fourth_in,
     load_sems, own_sem, spread_send, spread_recv, main_send, first_recv, second_recv,
     side_send, third_recv, fourth_recv,
 ):
@@ -42,9 +44,15 @@
     ]
     for load in label_loads:
         load.start()
+    first_target = lax.rem(x + ORDER[0], SIDE)
+    slab = [lax.rem(first_target + n, SLABS) for n in range(SLABS)]
     int_loads = [
-        pltpu.make_async_copy(ints_hbm.at[k], raw.at[k], load_sems.at[k])
-        for k in range(K_LOCAL)
+        pltpu.make_async_copy(
+            ints_hbm.at[:, :, pl.ds(pl.multiple_of(slab[n] * 16, 16), 16), :],
+            raw.at[n],
+            load_sems.at[n],
+        )
+        for n in range(SLABS)
     ]
     for load in int_loads:
         load.start()
@@ -71,15 +79,17 @@
                 barrier, inc=1, device_id=along(axis, step), device_id_type=MESH
             )
     lax.fori_loop(1, WIDE, greet, 0)
-    for k in range(K_LOCAL):
-        int_loads[k].wait()
-
-        def turn(step, carry, k=k):
+    def turn_slab(n):
+        int_loads[n].wait()
+        j = slab[n] * 16
+
+        def turn(step, carry):
             c = pl.multiple_of(step * 16, 16)
-            to = pl.multiple_of(k * SLOTS + step * 16, 16)
-            for q in range(5):
-                block = raw[k, pl.ds(c, 16), 16 * q : 16 * q + 16, :]
-                weights[16 * q : 16 * q + 16, pl.ds(to, 16), :] = jnp.swapaxes(block, 0, 1)
+            for k in range(K_LOCAL):
+                to = pl.multiple_of(k * SLOTS + step * 16, 16)
+                weights[pl.ds(j, 16), pl.ds(to, 16), :] = jnp.swapaxes(
+                    raw[n, k, pl.ds(c, 16), :, :], 0, 1
+                )
             return carry
 
         lax.fori_loop(0, SLOTS // 16, turn, 0)
@@ -101,9 +111,10 @@
             for place in range(4):
                 at = pl.multiple_of(target_group(chunk, place) * GROUP, GROUP)
                 block = amps[pl.ds(at, GROUP), k, :, :].reshape(16, SLOTS)
-                rows[chunk, 16 * place : 16 * place + 16, SLOTS * k : SLOTS * k + SLOTS] = (
-                    jnp.where(valid, to_f32(block), 0.0).astype(BF16)
-                )
+                at = chunk * 64 + place * 16
+                rows[at : at + 16, SLOTS * k : SLOTS * k + SLOTS] = jnp.where(
+                    valid, to_f32(block), 0.0
+                ).astype(BF16)
 
     sent = []
 
@@ -120,49 +131,51 @@
         sent.append(copy)
         return copy
 
-    def multiply(chunk):
-        for dx in (2, 1, 3, 0):
-
-            def pair(t, carry, dx=dx):
-                pieces = []
-                ways = (2 + t, 1 - t)
-                for dy in ways:
-                    target = lax.rem(x + dx, SIDE) * SIDE + lax.rem(y + dy, SIDE)
-                    pieces += [weights[target * J_LOCAL + j] for j in range(J_LOCAL)]
-                product = jnp.dot(
-                    rows[chunk], jnp.concatenate(pieces, axis=1), preferred_element_type=F32
-                ).astype(BF16)
-                for n, dy in enumerate(ways):
-                    for j in range(J_LOCAL):
-                        at = (n * J_LOCAL + j) * SLOTS
-                        part[chunk, 0, dx, dy, j] = product[:32, at : at + SLOTS]
-                        part[chunk, 1, dy, dx, j] = product[32:, at : at + SLOTS]
-                return carry
-
-            lax.fori_loop(0, 2, pair, 0)
-            base = chunk * 16
-            if dx == 2:
-                for d, half in ((0, 0), (1, 2)):
-                    send(
-                        part.at[chunk, 0, 2, pl.ds(half, 2)], first_in.at[chunk, 0, d],
-                        main_send, base + d, first_recv.at[chunk, 0, d], along(0, 1 - 2 * d),
-                    )
-            if dx in (1, 3):
-                d, half = (0, 2) if dx == 1 else (1, 0)
+    def multiply(dx):
+        def pair(t, carry):
+            pieces = []
+            ways = (2 + t, 1 - t)
+            for dy in ways:
+                target = lax.rem(x + dx, SIDE) * SIDE + lax.rem(y + dy, SIDE)
+                pieces += [weights[target * J_LOCAL + j] for j in range(J_LOCAL)]
+            product = jnp.dot(
+                rows[...], jnp.concatenate(pieces, axis=1), preferred_element_type=F32
+            ).astype(BF16)
+            for n, dy in enumerate(ways):
+                for j in range(J_LOCAL):
+                    at = (n * J_LOCAL + j) * SLOTS
+                    for chunk in range(2):
+                        top = chunk * 64
+                        part[chunk, 0, dx, dy, j] = product[top : top + 32, at : at + SLOTS]
+                        part[chunk, 1, dy, dx, j] = product[top + 32 : top + 64, at : at + SLOTS]
+            return carry
+
+        lax.fori_loop(0, 2, pair, 0)
+
+    def send_parts(chunk, dx):
+        base = chunk * 16
+        if dx == 2:
+            for d, half in ((0, 0), (1, 2)):
                 send(
-                    part.at[chunk, 0, dx, pl.ds(half, 2)],
-                    second_in.at[chunk, 0, d, pl.ds(half, 2)],
-                    main_send, base + 2 + d, second_recv.at[chunk, 0, d, 0], along(0, 1 - 2 * d),
+                    part.at[chunk, 0, 2, pl.ds(half, 2)], first_in.at[chunk, 0, d],
+                    main_send, base + d, first_recv.at[chunk, 0, d], along(0, 1 - 2 * d),
                 )
-            d = 0 if dx < 2 else 1
+        if dx in (1, 3):
+            d, half = (0, 2) if dx == 1 else (1, 0)
             send(
-                part.at[chunk, 1, 2, dx], first_in.at[chunk, 1, d, dx % 2],
-                main_send, base + 4 + dx, first_recv.at[chunk, 1, d], along(1, 1 - 2 * d),
+                part.at[chunk, 0, dx, pl.ds(half, 2)],
+                second_in.at[chunk, 0, d, pl.ds(half, 2)],
+                main_send, base + 2 + d, second_recv.at[chunk, 0, d, 0], along(0, 1 - 2 * d),
             )
-            send(
-                part.at[chunk, 1, 1 if d else 3, dx], second_in.at[chunk, 1, 1 - d, dx],
-                main_send, base + 8 + dx, second_recv.at[chunk, 1, 1 - d, 0], along(1, 2 * d - 1),
-            )
+        d = 0 if dx < 2 else 1
+        send(
+            part.at[chunk, 1, 2, dx], first_in.at[chunk, 1, d, dx % 2],
+            main_send, base + 4 + dx, first_recv.at[chunk, 1, d], along(1, 1 - 2 * d),
+        )
+        send(
+            part.at[chunk, 1, 1 if d else 3, dx], second_in.at[chunk, 1, 1 - d, dx],
+            main_send, base + 8 + dx, second_recv.at[chunk, 1, 1 - d, 0], along(1, 2 * d - 1),
+        )
 
     def wait_for(buffer, sem):
         pltpu.make_async_remote_copy(
@@ -238,33 +251,45 @@
             for d in range(2):
                 for h in range(2):
                     wait_for(fourth_in.at[chunk, way, d, h], fourth_recv.at[chunk, way, d, h])
+            bases, own_group = [], []
             for h in range(2):
                 place = 2 * way + h
                 base = pl.multiple_of(target_group(chunk, place) * GROUP, GROUP)
+                bases.append(base)
+                own_group.append(CHUNKS[chunk][place] == 0)
+                row_count = jnp.zeros_like(row)
+                for n in range(GROUP):
+                    row_count = jnp.where(row >> 1 == n, count_of(base + n), row_count)
+                row_valid = 2 * wide + (row & 1) < row_count
                 for j in range(J_LOCAL):
                     total = (
                         to_f32(mid[chunk, way, 0, h, j])
                         + to_f32(fourth_in[chunk, way, 0, h, j])
                         + to_f32(fourth_in[chunk, way, 1, h, j])
                     )
-                    total = jnp.where(lane < count_of(rep * J_LOCAL + j), total, 0.0)
-                    blocks[pl.ds(base, GROUP), j, :, :] = total.astype(BF16).reshape(GROUP, 2, SLOTS)
-                near = CHUNKS[chunk][place] == 0
-                inside = wide - group * GROUP
-
-                def push(step, carry, base=base, near=near):
-                    peer = base + (lax.rem(inside + step, GROUP) if near else step)
-                    pltpu.make_async_remote_copy(
-                        src_ref=blocks.at[peer],
-                        dst_ref=blocks_in.at[wide],
-                        send_sem=spread_send,
-                        recv_sem=spread_recv.at[chunk],
-                        device_id={"wide": peer, "rep": rep},
-                        device_id_type=MESH,
-                    ).start()
-                    return carry
-
-                lax.fori_loop(1 if near else 0, GROUP, push, 0)
+                    valid = row_valid & (lane < count_of(rep * J_LOCAL + j))
+                    total = jnp.where(valid, total, 0.0).astype(BF16)
+                    blocks[pl.ds(base, GROUP), j, :, :] = total.reshape(GROUP, 2, SLOTS)
+            inside = wide - group * GROUP
+
+            def push_to(peer):
+                pltpu.make_async_remote_copy(
+                    src_ref=blocks.at[peer],
+                    dst_ref=blocks_in.at[wide],
+                    send_sem=spread_send,
+                    recv_sem=spread_recv.at[chunk],
+                    device_id={"wide": peer, "rep": rep},
+                    device_id_type=MESH,
+                ).start()
+
+            def push(step, carry, bases=bases, own_group=own_group):
+                for base, near in zip(bases, own_group):
+                    push_to(base + (lax.rem(inside + step, GROUP) if near else step))
+                return carry
+
+            if own_group[1]:
+                push_to(bases[0])
+            lax.fori_loop(1 if own_group[1] else 0, GROUP, push, 0)
 
     def blocks_copy(many, sem):
         return pltpu.make_async_remote_copy(
@@ -276,26 +301,21 @@
             device_id_type=MESH,
         )
 
-    def assemble(chunk):
-        blocks_copy(32 - chunk, spread_recv.at[chunk]).wait_recv()
-        row_count = count_of(wide)
-        for away in CHUNKS[chunk]:
-            source = lax.rem(group - away + GROUP, GROUP)
-            at = pl.multiple_of(source * GROUP, GROUP)
-            to = pl.multiple_of(source * 16, 16)
-            for j in range(J_LOCAL):
-                block = blocks_in[pl.ds(at, GROUP), j, :, :].reshape(16, SLOTS)
-                out_ref[j, pl.ds(to, 16), :] = jnp.where(
-                    row + to < row_count, to_f32(block), 0.0
-                ).astype(BF16)
-
     amps_load.wait()
     gather_rows(0)
     gather_rows(1)
-    pl.semaphore_wait(barrier, WIDE - 1 + 4)
-    multiply(0)
+    ready = 0
+    for dx, needed in zip(ORDER, (2, 4, 5, 5)):
+        for n in range(ready, needed):
+            turn_slab(n)
+        ready = needed
+        multiply(dx)
+        if dx == ORDER[0]:
+            pl.semaphore_wait(barrier, WIDE - 1 + 4)
+        send_parts(0, dx)
     pass_on(0)
-    multiply(1)
+    for dx in ORDER:
+        send_parts(1, dx)
     turn_corner(0)
     pass_on(1)
     pass_on_side(0)
@@ -305,31 +325,29 @@
     spread(1)
     own = pltpu.make_async_copy(blocks.at[wide], blocks_in.at[wide], own_sem)
     own.start()
-    assemble(0)
     own.wait()
-    assemble(1)
-
-    blocks_copy(WIDE - 1, spread_recv.at[0]).wait_send()
     for copy in sent:
         copy.wait_send()
+    blocks_copy(WIDE - 1, spread_recv.at[0]).wait_send()
+    blocks_copy(WIDE // 2, spread_recv.at[0]).wait_recv()
+    blocks_copy(WIDE // 2 - 1, spread_recv.at[1]).wait_recv()
 
 
 def body(amplitudes, integrals, occ_irrep, vir_count):
     dma = pltpu.SemaphoreType.DMA
     out = pl.pallas_call(
         kernel,
-        out_shape=jax.ShapeDtypeStruct((J_LOCAL, SLOTS, SLOTS), BF16),
+        out_shape=jax.ShapeDtypeStruct((WIDE, J_LOCAL, 2, SLOTS), BF16),
         in_specs=[pl.BlockSpec(memory_space=pltpu.HBM)] * 4,
-        out_specs=pl.BlockSpec(memory_space=pltpu.VMEM),
+        out_specs=pl.BlockSpec(memory_space=pl.ANY),
         scratch_shapes=[
             pltpu.SMEM((80,), jnp.int32),
             pltpu.SMEM((8,), jnp.int32),
             pltpu.VMEM((WIDE, K_LOCAL, 2, SLOTS), BF16),
             pltpu.VMEM((WIDE, J_LOCAL, 2, SLOTS), BF16),
-            pltpu.VMEM((WIDE, K_LOCAL, 2, SLOTS), BF16),
-            pltpu.VMEM((K_LOCAL, SLOTS, 80, SLOTS), BF16),
+            pltpu.VMEM((SLABS, K_LOCAL, SLOTS, 16, SLOTS), BF16),
             pltpu.VMEM((80, K_LOCAL * SLOTS, SLOTS), BF16),
-            pltpu.VMEM((2, 64, K_LOCAL * SLOTS), BF16),
+            pltpu.VMEM((128, K_LOCAL * SLOTS), BF16),
             pltpu.VMEM((2, 2, 4, 4, J_LOCAL, 32, SLOTS), BF16),
             pltpu.VMEM((2, 2, 2, 2, J_LOCAL, 32, SLOTS), BF16),
             pltpu.VMEM((2, 2, 2, 4, J_LOCAL, 32, SLOTS), BF16),
@@ -354,7 +372,7 @@
             flops=2 * 128 * 640 * 10240, bytes_accessed=14 * 2**20, transcendentals=0
         ),
     )(amplitudes, integrals, occ_irrep, vir_count)
-    return out.transpose(1, 0, 2)[None]
+    return out.transpose(0, 2, 1, 3).reshape(1, 2 * WIDE, J_LOCAL, SLOTS)
 
 
 def solution(mesh):

time: 68.3 us -> 67.5 us (0.988)
  Pallas kernels: 66.5 us -> 65.5 us
    transpose x0 -> x1, local copies, waits for them, and re-layouts: none -> 1.7 us  [body(): return out.transpose(0, 2, 1, 3).reshape(1, 2 * WIDE, J_LOCAL, SLOTS)]
    unnamed x1 -> x0, local copies, waits for them, and re-layouts: 1.59 us -> none
    pallas_call x1, Pallas kernels: 66.5 us -> 65.5 us  [body(): pl.pallas_call(kernel, out_shape=jax.ShapeDtypeStruct((WIDE, J_LOCAL, 2,...]
where the time goes in v3:
time: 67.5 us; the launch traced here: 67.2 us
  Pallas kernels  65.5 us (97%)
  local copies, waits for them, and re-layouts  1.7 us (3%)
    pallas_call x1, Pallas kernels, body(): pl.pallas_call(kernel, out_shape=jax.ShapeDtypeStruct((WIDE, J_LOCAL, 2,...  65.5 us
    transpose x1, local copies, waits for them, and re-layouts, body(): return out.transpose(0, 2, 1, 3).reshape(1, 2 * WIDE, J_LOCAL, SLOTS)  1.7 us

profile of v3, /device:TPU:1, one launch (start us, length us, event | category | flops | bytes accessed | tf_op | source)
XLA Modules:
  0.0 67.2 jit_solution(2959716822695586569)
XLA Ops:
  0.0 65.5 %shard_map.46 = bf16[64,5,2,128]{3,2,1,0:T(2,128)(2,1)} custom-call(bf16[64,5,2,128]{3,2,1,0:T(2,128)(2,1)} %amps_hbm.1, bf16[5,128,80,128]{3,2,1,0:T(8,128)(2,1)} %ints_hbm.1, s32[80]{0:T(128)} %occ_hbm.1, s32[8]{0:T(128)} %vir_hbm.1), custom_call_target="tpu_custom_call" | custom-call | flops 1677721600 | bytes 14680064 | tf_op jit(solution)/shard_map/pallas_call | solution.py:338
  65.5 1.7 %copy.5 = bf16[64,2,5,128]{3,1,0,2:T(2,128)(2,1)} copy(bf16[64,2,5,128]{3,1,2,0:T(2,128)(2,1)} %bitcast.2) | data formatting | bytes 327680 | tf_op jit(solution)/shard_map/transpose | solution.py:375

commit v4 on v3

--- a/solution.py
+++ b/solution.py
@@ -29,7 +29,7 @@
     amps_hbm, ints_hbm, occ_hbm, vir_hbm, blocks_in,
     occ_ref, vir_ref, amps, blocks, raw, weights, rows, part, first_in, second_in, mid, third_in, fourth_in,
     load_sems, own_sem, spread_send, spread_recv, main_send, first_recv, second_recv,
-    side_send, third_recv, fourth_recv,
+    side_send, third_recv, fourth_recv, relay_one, relay_two,
 ):
     wide = lax.axis_index("wide")
     rep = lax.axis_index("rep")
@@ -65,20 +65,32 @@
         return {"wide": wide, "rep": other}
 
     barrier = pltpu.get_barrier_semaphore()
+    inside = wide - group * GROUP
 
     def greet(step, carry):
-        peer = lax.rem(wide + WIDE // 2 + (1 - 2 * (step % 2)) * (step // 2) + WIDE, WIDE)
+        place = lax.rem(GROUP + inside + step, 3 * GROUP)
+        peer = lax.rem(group * GROUP + place - GROUP + WIDE, WIDE)
         pl.semaphore_signal(
             barrier, inc=1, device_id={"wide": peer, "rep": rep}, device_id_type=MESH
         )
         return carry
+
+    def tell(relay, groups):
+        for away in (groups, -groups):
+            peer = lax.rem(wide + away * GROUP + WIDE, WIDE)
+            pl.semaphore_signal(
+                relay, inc=1, device_id={"wide": peer, "rep": rep}, device_id_type=MESH
+            )
 
     for axis in range(2):
         for step in (1, -1):
             pl.semaphore_signal(
                 barrier, inc=1, device_id=along(axis, step), device_id_type=MESH
             )
-    lax.fori_loop(1, WIDE, greet, 0)
+    lax.fori_loop(1, 3 * GROUP, greet, 0)
+    pl.semaphore_wait(barrier, 3 * GROUP - 1 + 4)
+    tell(relay_one, 1)
+
     def turn_slab(n):
         int_loads[n].wait()
         j = slab[n] * 16
@@ -270,7 +282,6 @@
                     valid = row_valid & (lane < count_of(rep * J_LOCAL + j))
                     total = jnp.where(valid, total, 0.0).astype(BF16)
                     blocks[pl.ds(base, GROUP), j, :, :] = total.reshape(GROUP, 2, SLOTS)
-            inside = wide - group * GROUP
 
             def push_to(peer):
                 pltpu.make_async_remote_copy(
@@ -310,15 +321,17 @@
             turn_slab(n)
         ready = needed
         multiply(dx)
+        send_parts(0, dx)
         if dx == ORDER[0]:
-            pl.semaphore_wait(barrier, WIDE - 1 + 4)
-        send_parts(0, dx)
+            pl.semaphore_wait(relay_one, 2)
+            tell(relay_two, 2)
     pass_on(0)
     for dx in ORDER:
         send_parts(1, dx)
     turn_corner(0)
     pass_on(1)
     pass_on_side(0)
+    pl.semaphore_wait(relay_two, 2)
     spread(0)
     turn_corner(1)
     pass_on_side(1)
@@ -364,6 +377,8 @@
             dma((24,)),
             dma((2, 2, 2)),
             dma((2, 2, 2, 2)),
+            pltpu.SemaphoreType.REGULAR,
+            pltpu.SemaphoreType.REGULAR,
         ],
         compiler_params=pltpu.CompilerParams(
             collective_id=0, has_side_effects=True, vmem_limit_bytes=63 * 2**20

time: 67.5 us -> 68.9 us (1.021)
  the two profiles are of different devices: /device:TPU:1 before, /device:TPU:67 now
where the time goes in v4:
time: 68.9 us; the launch traced here: 68.8 us
  Pallas kernels  67.1 us (97%)
  local copies, waits for them, and re-layouts  1.7 us (2%)
    pallas_call x1, Pallas kernels, body(): pl.pallas_call(kernel, out_shape=jax.ShapeDtypeStruct((WIDE, J_LOCAL, 2,...  67.1 us
    transpose x1, local copies, waits for them, and re-layouts, body(): return out.transpose(0, 2, 1, 3).reshape(1, 2 * WIDE, J_LOCAL, SLOTS)  1.7 us

profile of v4, /device:TPU:67, one launch (start us, length us, event | category | flops | bytes accessed | tf_op | source)
XLA Modules:
  0.0 68.8 jit_solution(16206559514306999734)
XLA Ops:
  0.0 67.1 %shard_map.46 = bf16[64,5,2,128]{3,2,1,0:T(2,128)(2,1)} custom-call(bf16[64,5,2,128]{3,2,1,0:T(2,128)(2,1)} %amps_hbm.1, bf16[5,128,80,128]{3,2,1,0:T(8,128)(2,1)} %ints_hbm.1, s32[80]{0:T(128)} %occ_hbm.1, s32[8]{0:T(128)} %vir_hbm.1), custom_call_target="tpu_custom_call" | custom-call | flops 1677721600 | bytes 14680064 | tf_op jit(solution)/shard_map/pallas_call | solution.py:351
  67.1 1.7 %copy.5 = bf16[64,2,5,128]{3,1,0,2:T(2,128)(2,1)} copy(bf16[64,2,5,128]{3,1,2,0:T(2,128)(2,1)} %bitcast.2) | data formatting | bytes 327680 | tf_op jit(solution)/shard_map/transpose | solution.py:390

commit v5 on v4

--- a/solution.py
+++ b/solution.py
@@ -322,19 +322,18 @@
         ready = needed
         multiply(dx)
         send_parts(0, dx)
+        send_parts(1, dx)
         if dx == ORDER[0]:
             pl.semaphore_wait(relay_one, 2)
             tell(relay_two, 2)
     pass_on(0)
-    for dx in ORDER:
-        send_parts(1, dx)
+    pass_on(1)
     turn_corner(0)
-    pass_on(1)
+    turn_corner(1)
     pass_on_side(0)
+    pass_on_side(1)
     pl.semaphore_wait(relay_two, 2)
     spread(0)
-    turn_corner(1)
-    pass_on_side(1)
     spread(1)
     own = pltpu.make_async_copy(blocks.at[wide], blocks_in.at[wide], own_sem)
     own.start()

time: 68.9 us -> 68.4 us (level)
  the two profiles are of different devices: /device:TPU:67 before, /device:TPU:1 now
where the time goes in v5:
time: 68.4 us; the launch traced here: 68.3 us
  Pallas kernels  66.5 us (97%)
  local copies, waits for them, and re-layouts  1.7 us (2%)
    pallas_call x1, Pallas kernels, body(): pl.pallas_call(kernel, out_shape=jax.ShapeDtypeStruct((WIDE, J_LOCAL, 2,...  66.5 us
    transpose x1, local copies, waits for them, and re-layouts, body(): return out.transpose(0, 2, 1, 3).reshape(1, 2 * WIDE, J_LOCAL, SLOTS)  1.7 us

profile of v5, /device:TPU:1, one launch (start us, length us, event | category | flops | bytes accessed | tf_op | source)
XLA Modules:
  0.0 68.3 jit_solution(7415606648308615525)
XLA Ops:
  0.0 66.5 %shard_map.46 = bf16[64,5,2,128]{3,2,1,0:T(2,128)(2,1)} custom-call(bf16[64,5,2,128]{3,2,1,0:T(2,128)(2,1)} %amps_hbm.1, bf16[5,128,80,128]{3,2,1,0:T(8,128)(2,1)} %ints_hbm.1, s32[80]{0:T(128)} %occ_hbm.1, s32[8]{0:T(128)} %vir_hbm.1), custom_call_target="tpu_custom_call" | custom-call | flops 1677721600 | bytes 14680064 | tf_op jit(solution)/shard_map/pallas_call | solution.py:350
  66.6 1.7 %copy.5 = bf16[64,2,5,128]{3,1,0,2:T(2,128)(2,1)} copy(bf16[64,2,5,128]{3,1,2,0:T(2,128)(2,1)} %bitcast.2) | data formatting | bytes 327680 | tf_op jit(solution)/shard_map/transpose | solution.py:389

commit v6 on v5

--- a/solution.py
+++ b/solution.py
@@ -27,9 +27,9 @@
 
 def kernel(
     amps_hbm, ints_hbm, occ_hbm, vir_hbm, blocks_in,
-    occ_ref, vir_ref, amps, blocks, raw, weights, rows, part, first_in, second_in, mid, third_in, fourth_in,
+    occ_ref, vir_ref, amps, blocks, raw, weights, rows, part, first_in, second_in, mid, side_in,
     load_sems, own_sem, spread_send, spread_recv, main_send, first_recv, second_recv,
-    side_send, third_recv, fourth_recv, relay_one, relay_two,
+    side_send, side_recv, relay_one, relay_two,
 ):
     wide = lax.axis_index("wide")
     rep = lax.axis_index("rep")
@@ -83,12 +83,12 @@
             )
 
     for axis in range(2):
-        for step in (1, -1):
+        for step in (1, 2, 3):
             pl.semaphore_signal(
                 barrier, inc=1, device_id=along(axis, step), device_id_type=MESH
             )
     lax.fori_loop(1, 3 * GROUP, greet, 0)
-    pl.semaphore_wait(barrier, 3 * GROUP - 1 + 4)
+    pl.semaphore_wait(barrier, 3 * GROUP - 1 + 6)
     tell(relay_one, 1)
 
     def turn_slab(n):
@@ -227,42 +227,18 @@
                 ).astype(BF16)
                 mid[chunk, way, ds, 0] = total[:, :16]
                 mid[chunk, way, ds, 1] = total[:, 16:]
-                base = chunk * 12 + way * 6
                 axis = 1 - way
-                if ds == 2:
-                    for d in range(2):
-                        send(
-                            mid.at[chunk, way, 2, d], third_in.at[chunk, way, d],
-                            side_send, base + d, third_recv.at[chunk, way, d],
-                            along(axis, 1 - 2 * d),
-                        )
-                if ds in (1, 3):
-                    d, h = (0, 1) if ds == 1 else (1, 0)
+                if ds:
                     send(
-                        mid.at[chunk, way, ds, h], fourth_in.at[chunk, way, d, h],
-                        side_send, base + 2 + d, fourth_recv.at[chunk, way, d, h],
-                        along(axis, 1 - 2 * d),
+                        mid.at[chunk, way, ds], side_in.at[chunk, way, ds - 1],
+                        side_send, chunk * 6 + way * 3 + ds - 1,
+                        side_recv.at[chunk, way, ds - 1], along(axis, ds),
                     )
-
-    def pass_on_side(chunk):
-        for way in range(2):
-            for d in range(2):
-                ds = 1 if d == 0 else 3
-                wait_for(third_in.at[chunk, way, d], third_recv.at[chunk, way, d])
-                mid[chunk, way, ds, d] = (
-                    to_f32(mid[chunk, way, ds, d]) + to_f32(third_in[chunk, way, d])
-                ).astype(BF16)
-                send(
-                    mid.at[chunk, way, ds, d], fourth_in.at[chunk, way, d, d],
-                    side_send, chunk * 12 + way * 6 + 4 + d, fourth_recv.at[chunk, way, d, d],
-                    along(1 - way, 1 - 2 * d),
-                )
 
     def spread(chunk):
         for way in range(2):
-            for d in range(2):
-                for h in range(2):
-                    wait_for(fourth_in.at[chunk, way, d, h], fourth_recv.at[chunk, way, d, h])
+            for d in range(3):
+                wait_for(side_in.at[chunk, way, d], side_recv.at[chunk, way, d])
             bases, own_group = [], []
             for h in range(2):
                 place = 2 * way + h
@@ -276,8 +252,9 @@
                 for j in range(J_LOCAL):
                     total = (
                         to_f32(mid[chunk, way, 0, h, j])
-                        + to_f32(fourth_in[chunk, way, 0, h, j])
-                        + to_f32(fourth_in[chunk, way, 1, h, j])
+                        + to_f32(side_in[chunk, way, 0, h, j])
+                        + to_f32(side_in[chunk, way, 1, h, j])
+                        + to_f32(side_in[chunk, way, 2, h, j])
                     )
                     valid = row_valid & (lane < count_of(rep * J_LOCAL + j))
                     total = jnp.where(valid, total, 0.0).astype(BF16)
@@ -330,8 +307,6 @@
     pass_on(1)
     turn_corner(0)
     turn_corner(1)
-    pass_on_side(0)
-    pass_on_side(1)
     pl.semaphore_wait(relay_two, 2)
     spread(0)
     spread(1)
@@ -364,8 +339,7 @@
             pltpu.VMEM((2, 2, 2, 2, J_LOCAL, 32, SLOTS), BF16),
             pltpu.VMEM((2, 2, 2, 4, J_LOCAL, 32, SLOTS), BF16),
             pltpu.VMEM((2, 2, 4, 2, J_LOCAL, 16, SLOTS), BF16),
-            pltpu.VMEM((2, 2, 2, J_LOCAL, 16, SLOTS), BF16),
-            pltpu.VMEM((2, 2, 2, 2, J_LOCAL, 16, SLOTS), BF16),
+            pltpu.VMEM((2, 2, 3, 2, J_LOCAL, 16, SLOTS), BF16),
             dma((K_LOCAL + 3,)),
             dma,
             dma,
@@ -373,9 +347,8 @@
             dma((32,)),
             dma((2, 2, 2)),
             dma((2, 2, 2, 2)),
-            dma((24,)),
-            dma((2, 2, 2)),
-            dma((2, 2, 2, 2)),
+            dma((12,)),
+            dma((2, 2, 3)),
             pltpu.SemaphoreType.REGULAR,
             pltpu.SemaphoreType.REGULAR,
         ],

time: 68.4 us -> 67.3 us (0.984)
  Pallas kernels: 66.5 us -> 65.5 us
    pallas_call x1, Pallas kernels: 66.5 us -> 65.5 us  [body(): pl.pallas_call(kernel, out_shape=jax.ShapeDtypeStruct((WIDE, J_LOCAL, 2,...]
where the time goes in v6:
time: 67.3 us; the launch traced here: 67.2 us
  Pallas kernels  65.5 us (97%)
  local copies, waits for them, and re-layouts  1.7 us (3%)
    pallas_call x1, Pallas kernels, body(): pl.pallas_call(kernel, out_shape=jax.ShapeDtypeStruct((WIDE, J_LOCAL, 2,...  65.5 us
    transpose x1, local copies, waits for them, and re-layouts, body(): return out.transpose(0, 2, 1, 3).reshape(1, 2 * WIDE, J_LOCAL, SLOTS)  1.7 us

profile of v6, /device:TPU:1, one launch (start us, length us, event | category | flops | bytes accessed | tf_op | source)
XLA Modules:
  0.0 67.2 jit_solution(9525914568952676993)
XLA Ops:
  0.0 65.5 %shard_map.46 = bf16[64,5,2,128]{3,2,1,0:T(2,128)(2,1)} custom-call(bf16[64,5,2,128]{3,2,1,0:T(2,128)(2,1)} %amps_hbm.1, bf16[5,128,80,128]{3,2,1,0:T(8,128)(2,1)} %ints_hbm.1, s32[80]{0:T(128)} %occ_hbm.1, s32[8]{0:T(128)} %vir_hbm.1), custom_call_target="tpu_custom_call" | custom-call | flops 1677721600 | bytes 14680064 | tf_op jit(solution)/shard_map/pallas_call | solution.py:325
  65.5 1.7 %copy.5 = bf16[64,2,5,128]{3,1,0,2:T(2,128)(2,1)} copy(bf16[64,2,5,128]{3,1,2,0:T(2,128)(2,1)} %bitcast.2) | data formatting | bytes 327680 | tf_op jit(solution)/shard_map/transpose | solution.py:362

commit v7 on v6

--- a/solution.py
+++ b/solution.py
@@ -299,16 +299,17 @@
         ready = needed
         multiply(dx)
         send_parts(0, dx)
-        send_parts(1, dx)
         if dx == ORDER[0]:
             pl.semaphore_wait(relay_one, 2)
             tell(relay_two, 2)
     pass_on(0)
+    for dx in ORDER:
+        send_parts(1, dx)
+    turn_corner(0)
     pass_on(1)
-    turn_corner(0)
-    turn_corner(1)
     pl.semaphore_wait(relay_two, 2)
     spread(0)
+    turn_corner(1)
     spread(1)
     own = pltpu.make_async_copy(blocks.at[wide], blocks_in.at[wide], own_sem)
     own.start()

time: 67.3 us -> 67.9 us (level)
  the two profiles are of different devices: /device:TPU:1 before, /device:TPU:35 now
where the time goes in v7:
time: 67.9 us; the launch traced here: 67.7 us
  Pallas kernels  66 us (97%)
  local copies, waits for them, and re-layouts  1.7 us (3%)
    pallas_call x1, Pallas kernels, body(): pl.pallas_call(kernel, out_shape=jax.ShapeDtypeStruct((WIDE, J_LOCAL, 2,...  66 us
    transpose x1, local copies, waits for them, and re-layouts, body(): return out.transpose(0, 2, 1, 3).reshape(1, 2 * WIDE, J_LOCAL, SLOTS)  1.7 us

profile of v7, /device:TPU:35, one launch (start us, length us, event | category | flops | bytes accessed | tf_op | source)
XLA Modules:
  0.0 67.7 jit_solution(8143515013279086886)
XLA Ops:
  0.0 66.0 %shard_map.46 = bf16[64,5,2,128]{3,2,1,0:T(2,128)(2,1)} custom-call(bf16[64,5,2,128]{3,2,1,0:T(2,128)(2,1)} %amps_hbm.1, bf16[5,128,80,128]{3,2,1,0:T(8,128)(2,1)} %ints_hbm.1, s32[80]{0:T(128)} %occ_hbm.1, s32[8]{0:T(128)} %vir_hbm.1), custom_call_target="tpu_custom_call" | custom-call | flops 1677721600 | bytes 14680064 | tf_op jit(solution)/shard_map/pallas_call | solution.py:326
  66.0 1.7 %copy.5 = bf16[64,2,5,128]{3,1,0,2:T(2,128)(2,1)} copy(bf16[64,2,5,128]{3,1,2,0:T(2,128)(2,1)} %bitcast.2) | data formatting | bytes 327680 | tf_op jit(solution)/shard_map/transpose | solution.py:363

commit v8 on v6

--- a/solution.py
+++ b/solution.py
@@ -18,7 +18,7 @@
 J_LOCAL = 5
 SLABS = 5
 ORDER = (2, 3, 1, 0)
-CHUNKS = ((3, -3, 4, -2), (2, -1, 1, 0))
+CHUNKS = ((4, -2, 3, -3), (2, -1, 1, 0))
 
 
 def to_f32(value):
@@ -201,8 +201,8 @@
                 dp, half = (1, 0) if d == 0 else (3, 2)
                 wait_for(first_in.at[chunk, way, d], first_recv.at[chunk, way, d])
                 part[chunk, way, dp, half : half + 2] = (
-                    to_f32(part[chunk, way, dp, half : half + 2]) + to_f32(first_in[chunk, way, d])
-                ).astype(BF16)
+                    part[chunk, way, dp, half : half + 2] + first_in[chunk, way, d]
+                )
                 send(
                     part.at[chunk, way, dp, pl.ds(half, 2)],
                     second_in.at[chunk, way, d, pl.ds(half, 2)],

time: 67.3 us -> 65.7 us (0.976)
  Pallas kernels: 65.5 us -> 63.8 us
    pallas_call x1, Pallas kernels: 65.5 us -> 63.8 us  [body(): pl.pallas_call(kernel, out_shape=jax.ShapeDtypeStruct((WIDE, J_LOCAL, 2,...]
where the time goes in v8:
time: 65.7 us; the launch traced here: 65.5 us
  Pallas kernels  63.8 us (97%)
  local copies, waits for them, and re-layouts  1.7 us (3%)
    pallas_call x1, Pallas kernels, body(): pl.pallas_call(kernel, out_shape=jax.ShapeDtypeStruct((WIDE, J_LOCAL, 2,...  63.8 us
    transpose x1, local copies, waits for them, and re-layouts, body(): return out.transpose(0, 2, 1, 3).reshape(1, 2 * WIDE, J_LOCAL, SLOTS)  1.7 us

profile of v8, /device:TPU:1, one launch (start us, length us, event | category | flops | bytes accessed | tf_op | source)
XLA Modules:
  0.0 65.5 jit_solution(6417624475277588582)
XLA Ops:
  0.0 63.8 %shard_map.46 = bf16[64,5,2,128]{3,2,1,0:T(2,128)(2,1)} custom-call(bf16[64,5,2,128]{3,2,1,0:T(2,128)(2,1)} %amps_hbm.1, bf16[5,128,80,128]{3,2,1,0:T(8,128)(2,1)} %ints_hbm.1, s32[80]{0:T(128)} %occ_hbm.1, s32[8]{0:T(128)} %vir_hbm.1), custom_call_target="tpu_custom_call" | custom-call | flops 1677721600 | bytes 14680064 | tf_op jit(solution)/shard_map/pallas_call | solution.py:325
  63.8 1.7 %copy.5 = bf16[64,2,5,128]{3,1,0,2:T(2,128)(2,1)} copy(bf16[64,2,5,128]{3,1,2,0:T(2,128)(2,1)} %bitcast.2) | data formatting | bytes 327680 | tf_op jit(solution)/shard_map/transpose | solution.py:362
